TPU v7x, 32 devices: a whole 2x2x4 slice. The times are simulated.
32 devices in a mesh: dp: 4 (over z), expert: 8 (over y, x, core).
Axes of the slice: x: 2, y: 2, z: 4, core: 2. Of those that a mesh axis runs over, the one named last changes fastest.
Arguments:
- tokens: bfloat16 [2048, 4096], P('expert', 'dp'), may hold values from -6 to 6
- targets: bfloat16 [2048, 4096], P('expert', 'dp'), may hold values from -4 to 4
- expert_ids: int32 [2048, 2], P('expert'), may hold values from 0 to 7, all different within a row; in each aligned block of 256 rows (0 to 255, 256 to 511, ...) at most 128 rows name the same one
- gate_weights: float32 [2048, 2], P('expert'), may hold values from 0.2 to 1
- level_weights: float32 [2048], P('expert'), may hold values from 0.2 to 2
- w_gate: bfloat16 [8, 4096, 1024], P('expert', 'dp'), may hold values from -0.09375 to 0.09375
- w_up: bfloat16 [8, 4096, 1024], P('expert', 'dp'), may hold values from -0.09375 to 0.09375
- w_down: bfloat16 [8, 1024, 4096], P('expert', None, 'dp'), may hold values from -0.1875 to 0.1875
Outputs:
- mixed: bfloat16 [2048, 4096], P('expert', 'dp')
- token_grad: bfloat16 [2048, 4096], P('expert', 'dp')
- gate_grads: float32 [8, 4096, 1024], P('expert', 'dp')
- up_grads: float32 [8, 4096, 1024], P('expert', 'dp')
- down_grads: float32 [8, 1024, 4096], P('expert', None, 'dp')
Inputs may be any that keep to these rules, and one draw needn't show every extreme that they name: `expert_ids`: each row names two different experts. Among the rows of one device no expert is named more than 128 times, a bound that some block reaches.
All inputs are finite; a program needn't handle non-finite values.
Results may differ from a plain program's by a relative error of at most 0.0065.
Values may be sent and summed in bfloat16 or wider, within the bound.
A program may use at most 128 MiB of HBM per device.

v0:
```python
import jax
import jax.numpy as jnp
from jax import lax
from jax.sharding import PartitionSpec as P


def slot_ranks(routing, experts):
    listed = routing.reshape(routing.shape[0], -1)
    onehot = (listed[:, :, None] == jnp.arange(experts, dtype=jnp.int32)[None, None, :]).astype(
        jnp.int32
    )
    earlier = jnp.cumsum(onehot, axis=1) - onehot
    return jnp.sum(earlier * onehot, axis=2)


def contract(left, right, left_dim, right_dim):
    return lax.dot_general(
        left, right, (((left_dim,), (right_dim,)), ((), ())), preferred_element_type=jnp.float32
    )


def activate(gate_pre, up_pre):
    sigmoid_gate = jax.nn.sigmoid(gate_pre)
    return (sigmoid_gate, (gate_pre * sigmoid_gate * up_pre).astype(jnp.bfloat16))


def derivatives(hidden_grad, gate_pre, up_pre, sigmoid_gate):
    gate_delta = (
        hidden_grad * up_pre * sigmoid_gate * (1.0 + gate_pre * (1.0 - sigmoid_gate))
    ).astype(jnp.bfloat16)
    up_delta = (hidden_grad * gate_pre * sigmoid_gate).astype(jnp.bfloat16)
    return (gate_delta, up_delta)


def shards(tokens, targets, expert_ids, gate_weights, level_weights, w_gate, w_up, w_down):
    experts = lax.axis_size("expert")
    tok_rows = tokens.shape[0]
    quarter = tokens.shape[1]
    capacity = 4 * tok_rows // experts
    rows_all = experts * capacity
    gate_mat = w_gate[0]
    up_mat = w_up[0]
    down_mat = w_down[0]
    ranks = slot_ranks(expert_ids.reshape(1, tok_rows, 2), experts).reshape(-1)
    slot_rows = expert_ids.reshape(-1) * capacity + ranks
    spread = jnp.repeat(tokens, 2, axis=0)
    outgoing = jnp.zeros((rows_all, quarter), jnp.bfloat16).at[slot_rows].set(spread)
    arrived = lax.all_to_all(
        outgoing.reshape(experts, capacity, quarter),
        "expert",
        split_axis=0,
        concat_axis=0,
        tiled=True,
    ).reshape(rows_all, quarter)
    gate_pre, up_pre = lax.psum(
        (contract(arrived, gate_mat, 1, 0), contract(arrived, up_mat, 1, 0)), "dp"
    )
    sigmoid_gate, hidden = activate(gate_pre, up_pre)
    out_slots = (
        contract(hidden, down_mat, 1, 0).astype(jnp.bfloat16).reshape(experts, capacity, quarter)
    )
    returned = lax.all_to_all(out_slots, "expert", split_axis=0, concat_axis=0, tiled=True).reshape(
        rows_all, quarter
    )
    picked = returned[slot_rows].reshape(tok_rows, 2, quarter).astype(jnp.float32)
    combined = jnp.sum(gate_weights[:, :, None] * picked, axis=1)
    mixed = combined.astype(jnp.bfloat16)
    row_grad = level_weights[:, None] * (combined - targets.astype(jnp.float32))
    slot_grad = (
        (gate_weights[:, :, None] * row_grad[:, None, :])
        .astype(jnp.bfloat16)
        .reshape(2 * tok_rows, quarter)
    )
    grad_out = jnp.zeros((rows_all, quarter), jnp.bfloat16).at[slot_rows].set(slot_grad)
    grad_slots = lax.all_to_all(
        grad_out.reshape(experts, capacity, quarter),
        "expert",
        split_axis=0,
        concat_axis=0,
        tiled=True,
    ).reshape(rows_all, quarter)
    down_grad = contract(hidden, grad_slots, 0, 0)
    hidden_grad = lax.psum(contract(grad_slots, down_mat, 1, 1), "dp")
    gate_delta, up_delta = derivatives(hidden_grad, gate_pre, up_pre, sigmoid_gate)
    input_slots = (contract(gate_delta, gate_mat, 1, 1) + contract(up_delta, up_mat, 1, 1)).astype(
        jnp.bfloat16
    )
    gate_grad = contract(arrived, gate_delta, 0, 0)
    up_grad = contract(arrived, up_delta, 0, 0)
    input_back = lax.all_to_all(
        input_slots.reshape(experts, capacity, quarter),
        "expert",
        split_axis=0,
        concat_axis=0,
        tiled=True,
    ).reshape(rows_all, quarter)
    token_grad = jnp.sum(
        input_back[slot_rows].reshape(tok_rows, 2, quarter).astype(jnp.float32), axis=1
    ).astype(jnp.bfloat16)
    return (mixed, token_grad, gate_grad[None], up_grad[None], down_grad[None])


def solution(mesh):
    in_specs = (
        P("expert", "dp"),
        P("expert", "dp"),
        P("expert", None),
        P("expert", None),
        P("expert"),
        P("expert", "dp", None),
        P("expert", "dp", None),
        P("expert", None, "dp"),
    )
    out_specs = (
        P("expert", "dp"),
        P("expert", "dp"),
        P("expert", "dp", None),
        P("expert", "dp", None),
        P("expert", None, "dp"),
    )
    return jax.shard_map(shards, mesh=mesh, in_specs=in_specs, out_specs=out_specs, check_vma=False)
```

profile of v0, /device:TPU:0, one launch (start us, length us, event | category | flops | bytes accessed | tf_op | source)
XLA Modules:
  0.0 663.5 jit_solution(7966923062043029704)
XLA Ops:
  7.2 0.0 copy-start
  7.2 0.0 all-reduce.6.cloned.1.call-start
  7.2 0.8 broadcast_multiply_fusion
  8.1 0.8 copy.16
  8.9 0.1 copy.15
  9.0 0.1 mul.80
  9.2 0.1 eq.27
  9.3 1.1 reduce-window.6
  10.5 0.2 slice_reduce_fusion
  10.7 0.1 fusion.23
  10.8 1.6 broadcast_in_dim.8
  12.4 1.2 reshape.231
  13.6 4.8 scatter_custom_fusion
  18.4 31.9 %all_to_all.20 = bf16[8,128,1024]{2,1,0:T(8,128)(2,1)S(1)} all-to-all(bf16[8,128,1024]{2,1,0:T(8,128)(2,1)} %bitcast.65), channel_id=1, replica_groups=mesh['dp'=4,'expert'=8] {'expert'}, dimensions={0} | all-to-all | bytes 4194304 | tf_op jit(solution)/shard_map/all_to_all | solution.py:48
  50.3 0.0 copy-done.14
  50.3 4.4 fusion.6
  54.7 0.0 copy-done.4
  54.7 0.0 copy-done.16
  54.7 4.4 fusion.10
  59.0 0.0 all-reduce.6.cloned.1.call-update
  59.1 291.0 %all-reduce.6.cloned.1.call-done = (f32[1024,1024]{1,0:T(8,128)}, f32[1024,1024]{1,0:T(8,128)}) async-done(((f32[1024,1024]{1,0:T(8,128)}, f32[1024,1024]{1,0:T(8,128)}), (f32[1024,1024]{1,0:T(8,128)}, f32[1024,1024]{1,0:T(8,128)})) %all-reduce.6.cloned.1.call-update) | async-done | bytes 8388624 | tf_op jit(solution)/shard_map/psum | solution.py:55
  350.1 4.8 multiply_convert_fusion.2
  354.9 0.0 copy-done
  355.0 0.0 copy-start.2
  355.0 3.7 fusion.12
  358.6 0.0 copy-done.2
  358.6 4.5 all-to-all-start.1
  363.1 0.2 all-reduce.4.cloned.1.call-start
  363.4 0.0 copy-done.12
  363.4 0.1 copy.14
  363.5 0.1 mul.85
  363.7 26.1 %all-to-all-done.1 = bf16[8,128,1024]{2,1,0:T(8,128)(2,1)} async-done(((bf16[8,128,1024]{2,1,0:T(8,128)(2,1)}), bf16[8,128,1024]{2,1,0:T(8,128)(2,1)}, u32[]{:S(2)}, u32[]{:S(2)}) %all-to-all-start.1) | async-done | bytes 2097184 | tf_op jit(solution)/shard_map/all_to_all | solution.py:62
  389.8 4.6 gather_fusion
  394.4 2.3 reshape.210
  396.7 4.3 multiply_reduce_fusion
  401.0 0.0 copy-done.11
  401.0 0.0 copy-done.13
  401.1 1.0 subtract_multiply_fusion
  402.1 2.0 mul.89
  404.1 3.6 mul.90
  407.8 5.2 scatter_custom_fusion.1
  413.0 30.3 %all_to_all.21 = bf16[8,128,1024]{2,1,0:T(8,128)(2,1)S(1)} all-to-all(bf16[8,128,1024]{2,1,0:T(8,128)(2,1)} %bitcast.64), channel_id=1, replica_groups=mesh['dp'=4,'expert'=8] {'expert'}, dimensions={0} | all-to-all | bytes 4194304 | tf_op jit(solution)/shard_map/all_to_all | solution.py:75
  443.3 1.3 copy-done.6
  444.6 4.4 fusion
  449.1 0.0 all-reduce.4.cloned.1.call-update
  449.1 152.3 %all-reduce.4.cloned.1.call-done = f32[1024,1024]{1,0:T(8,128)} async-done(((f32[1024,1024]{1,0:T(8,128)}), f32[1024,1024]{1,0:T(8,128)}) %all-reduce.4.cloned.1.call-update) | async-done | bytes 4194320 | tf_op jit(solution)/shard_map/psum | solution.py:83
  601.4 6.0 multiply_convert_fusion.1
  607.5 0.0 copy-start.7
  607.5 0.0 copy-start.9
  607.5 0.0 copy-start.17
  607.5 2.4 fusion.4
  610.0 0.6 copy-done.17
  610.6 3.7 add_convert_fusion
  614.3 4.7 all-to-all-start.3
  619.0 0.0 copy-start.5
  619.0 0.0 copy-start.10
  619.1 6.1 convolution_bitcast_fusion
  625.2 0.0 copy-done.5
  625.2 4.4 convolution_bitcast_fusion.2
  629.6 4.4 convolution_bitcast_fusion.1
  634.1 11.6 %all-to-all-done.3 = bf16[8,128,1024]{2,1,0:T(8,128)(2,1)} async-done(((bf16[8,128,1024]{2,1,0:T(8,128)(2,1)}), bf16[8,128,1024]{2,1,0:T(8,128)(2,1)}, u32[]{:S(2)}, u32[]{:S(2)}) %all-to-all-start.3) | async-done | bytes 2097184 | tf_op jit(solution)/shard_map/all_to_all | solution.py:90
  645.7 4.7 gather_fusion.1
  650.4 1.2 reshape.209
  651.7 4.6 reduce_sum.35
  (23 shorter events, 0.1 us)
Async XLA Ops:
  7.2 347.8 %copy-start = (bf16[1,1024,1024]{2,1,0:T(8,128)(2,1)S(1)}, bf16[1,1024,1024]{2,1,0:T(8,128)(2,1)}, u32[]{:S(2)}) copy-start(bf16[1,1024,1024]{2,1,0:T(8,128)(2,1)} %param.15) | copy-start | bytes 6291460
  7.2 342.9 %all-reduce.6.cloned.1.call-start = ((), (), s32[]{:S(2)}) async-start(), calls=%async_computation.5 | async-start | bytes 16777216 | tf_op jit(solution)/shard_map/psum | solution.py:55
  18.4 31.9 %copy-start.14 = (bf16[1,1024,1024]{2,1,0:T(8,128)(2,1)S(1)}, bf16[1,1024,1024]{2,1,0:T(8,128)(2,1)}, u32[]{:S(2)}) copy-start(bf16[1,1024,1024]{2,1,0:T(8,128)(2,1)} %param.14) | copy-start | bytes 6291460
  50.3 4.4 copy-start.4
  50.3 4.4 copy-start.16
  355.0 3.7 copy-start.2
  358.6 4.7 copy-start.12
  358.6 31.2 %all-to-all-start.1 = ((bf16[8,128,1024]{2,1,0:T(8,128)(2,1)}), bf16[8,128,1024]{2,1,0:T(8,128)(2,1)}, u32[]{:S(2)}, u32[]{:S(2)}) async-start(bf16[8,128,1024]{2,1,0:T(8,128)(2,1)} %bitcast.73), calls=%async_computation.1 | async-start | bytes 4194304 | tf_op jit(solution)/shard_map/all_to_all | solution.py:62
  363.1 238.3 %all-reduce.4.cloned.1.call-start = ((), (), s32[]{:S(2)}) async-start(), calls=%async_computation.4 | async-start | bytes 8388608 | tf_op jit(solution)/shard_map/psum | solution.py:83
  396.7 4.3 copy-start.11
  396.7 4.4 copy-start.13
  443.3 1.3 copy-start.6
  601.4 6.0 copy-start.15
  607.5 2.5 copy-start.7
  607.5 2.5 copy-start.9
  607.5 3.1 copy-start.17
  614.3 4.7 copy-start.3
  614.3 31.4 %all-to-all-start.3 = ((bf16[8,128,1024]{2,1,0:T(8,128)(2,1)}), bf16[8,128,1024]{2,1,0:T(8,128)(2,1)}, u32[]{:S(2)}, u32[]{:S(2)}) async-start(bf16[8,128,1024]{2,1,0:T(8,128)(2,1)} %bitcast.72), calls=%async_computation.3 | async-start | bytes 4194304 | tf_op jit(solution)/shard_map/all_to_all | solution.py:90
  619.0 6.2 copy-start.5
  619.0 6.2 copy-start.10
  625.2 4.5 copy-start.8
  645.7 10.5 %copy-start.1 = (bf16[1,1024,1024]{2,1,0:T(8,128)(2,1)S(1)}, bf16[1,1024,1024]{2,1,0:T(8,128)(2,1)}, u32[]{:S(2)}) copy-start(bf16[1,1024,1024]{2,1,0:T(8,128)(2,1)} %param.15) | copy-start | bytes 6291460
Sparse Core Ops, SparseCore 0:
  59.2 290.8 all-reduce.5
  449.2 152.1 all-reduce.3
where the time goes:
time: 672 us; the launch traced here: 663 us
  waiting for transfers between devices  481 us (72%)
  blocking collectives  62.2 us (9%)
  matrix products  38 us (6%)
  local copies, waits for them, and re-layouts  29.9 us (4%)
  other arithmetic  28.1 us (4%)
  between operations  14.7 us (2%)
  starting transfers between devices  9.47 us (1%)
    psum x1, waiting for transfers between devices, shards(): lax.psum((contract(arrived, gate_mat, 1, 0), contract(arrived, up_mat, 1,...  291 us
    psum x1, waiting for transfers between devices, shards(): hidden_grad = lax.psum(contract(grad_slots, down_mat, 1, 1), 'dp')  152 us
    dot_general x9, matrix products, contract(): lax.dot_general(left, right, (((left_dim,), (right_dim,)), ((), ())), pre...  38 us
    all_to_all x1, blocking collectives, shards(): lax.all_to_all(outgoing.reshape(experts, capacity, quarter), 'expert', sp...  31.9 us
    all_to_all x1, blocking collectives, shards(): lax.all_to_all(grad_out.reshape(experts, capacity, quarter), 'expert', sp...  30.3 us
    all_to_all x1, waiting for transfers between devices, shards(): lax.all_to_all(out_slots, 'expert', split_axis=0, concat_axis=0, tiled=True)  26.1 us
  transfers between devices with their start and end apart: 4, of which 4 were waited for; matrix products, arithmetic and copies ran while one was open for 2% of the time, Pallas kernels for 0%

commit v1 on v0

v1 whole, which is shorter than its diff:
```python
import functools

import jax
import jax.numpy as jnp
from jax import lax
from jax.experimental import pallas as pl
from jax.experimental.pallas import tpu as pltpu
from jax.sharding import PartitionSpec as P

BF16 = jnp.bfloat16
F32 = jnp.float32
MESH = pl.DeviceIdType.MESH

DISPATCH, OUTPUT, GRAD, INPUT = range(4)
GATE, UP, HIDDEN, HIDDEN_GRAD, GATE_DELTA, UP_DELTA = range(6)


def contract(left, right, left_dim, right_dim):
    return lax.dot_general(
        left, right, (((left_dim,), (right_dim,)), ((), ())), preferred_element_type=F32
    )


def layer(
    n_z,
    n_e,
    cap,
    tok,
    tgt,
    slot_cols,
    slot_lanes,
    gate_w,
    level_w,
    w_gate,
    w_up,
    w_down,
    mixed,
    token_grad,
    gate_grad,
    up_grad,
    down_grad,
    stage,
    arrived,
    pre_out,
    pre_in,
    gate_own,
    up_own,
    hidden,
    returned,
    slot_grad,
    grads,
    grad_own,
    grad_in,
    gate_delta,
    up_delta,
    back,
    tiles,
    e_send,
    e_recv,
    z_send,
    z_recv,
    tile_sem,
):
    my_z = lax.axis_index("dp")
    my_e = lax.axis_index("expert")
    rows_all = n_e * cap
    shard = rows_all // n_z
    per_shard = n_e // n_z
    tok_rows = tok.shape[0]
    step = min(64, shard)

    def shard_rows(z):
        return pl.ds(pl.multiple_of(z * shard, shard), shard)

    def block_rows(e):
        return pl.ds(pl.multiple_of(e * cap, cap), cap)

    def e_copy(phase, landing, other, source):
        return pltpu.make_async_remote_copy(
            src_ref=stage.at[block_rows(other)],
            dst_ref=landing.at[block_rows(source)],
            send_sem=e_send.at[phase, other],
            recv_sem=e_recv.at[phase, source],
            device_id={"expert": other},
            device_id_type=MESH,
        )

    def send_blocks(phase, landing, z):
        for i in range(per_shard):
            other = z * per_shard + i

            @pl.when(other != my_e)
            def _():
                e_copy(phase, landing, other, my_e).start()

            @pl.when(other == my_e)
            def _():
                landing[block_rows(my_e), :] = stage[block_rows(my_e), :]

    def wait_blocks(phase, landing, z):
        for i in range(per_shard):
            other = z * per_shard + i

            @pl.when(other != my_e)
            def _():
                e_copy(phase, landing, other, other).wait_recv()

    def wait_sent(phase, landing):
        @pl.loop(0, n_e)
        def _(other):
            @pl.when(other != my_e)
            def _():
                e_copy(phase, landing, other, my_e).wait_send()

    def z_copy(phase, src, dst, z, source):
        return pltpu.make_async_remote_copy(
            src_ref=src,
            dst_ref=dst,
            send_sem=z_send.at[phase, z],
            recv_sem=z_recv.at[phase, source],
            device_id={"dp": z},
            device_id_type=MESH,
        )

    def gather_copy(phase, array, z, source):
        return z_copy(phase, array.at[shard_rows(source)], array.at[shard_rows(source)], z, source)

    def other_z(s):
        return lax.rem(my_z + s, n_z)

    barrier = pltpu.get_barrier_semaphore()

    @pl.loop(1, n_z)
    def _(s):
        pl.semaphore_signal(barrier, inc=1, device_id={"dp": other_z(s)}, device_id_type=MESH)

    @pl.loop(1, n_e)
    def _(s):
        pl.semaphore_signal(
            barrier, inc=1, device_id={"expert": lax.rem(my_e + s, n_e)}, device_id_type=MESH
        )

    pl.semaphore_wait(barrier, n_z + n_e - 2)

    def scatter_tile(z, k):
        slots = lax.broadcasted_iota(jnp.int32, (shard, tok_rows), 0) + z * shard
        return (slots == slot_lanes[k : k + 1, :]).astype(F32)

    def gather_matrix(k):
        slots = lax.broadcasted_iota(jnp.int32, (tok_rows, rows_all), 1)
        return (slots == slot_cols[:, k : k + 1]).astype(F32)

    @pl.loop(0, n_z)
    def _(s):
        z = other_z(s + 1)
        chosen = (scatter_tile(z, 0) + scatter_tile(z, 1)).astype(BF16)
        stage[shard_rows(z), :] = contract(chosen, tok[...], 1, 0).astype(BF16)
        send_blocks(DISPATCH, arrived, z)

    @pl.loop(1, n_z)
    def _(s):
        z = other_z(s)
        wait_blocks(DISPATCH, arrived, z)
        rows = arrived[shard_rows(z), :]
        pre_out[GATE, z] = contract(rows, w_gate[...], 1, 0).astype(BF16)
        z_copy(GATE, pre_out.at[GATE, z], pre_in.at[GATE, my_z], z, my_z).start()
        pre_out[UP, z] = contract(rows, w_up[...], 1, 0).astype(BF16)
        z_copy(UP, pre_out.at[UP, z], pre_in.at[UP, my_z], z, my_z).start()

    wait_blocks(DISPATCH, arrived, my_z)
    gate_own[...] = contract(arrived[shard_rows(my_z), :], w_gate[...], 1, 0)
    up_own[...] = contract(arrived[shard_rows(my_z), :], w_up[...], 1, 0)
    wait_sent(DISPATCH, arrived)

    @pl.loop(1, n_z)
    def _(s):
        z = other_z(s)
        for phase, own in ((GATE, gate_own), (UP, up_own)):
            z_copy(phase, pre_out.at[phase, z], pre_in.at[phase, z], z, z).wait_recv()

            @pl.loop(0, shard // step)
            def _(c):
                rows = pl.ds(pl.multiple_of(c * step, step), step)
                own[rows, :] = own[rows, :] + pre_in[phase, z, rows, :].astype(F32)

    @pl.loop(0, shard // step)
    def _(c):
        rows = pl.ds(pl.multiple_of(c * step, step), step)
        gate = gate_own[rows, :]
        value = gate * jax.nn.sigmoid(gate) * up_own[rows, :]
        target = pl.ds(pl.multiple_of(my_z * shard + c * step, step), step)
        hidden[target, :] = value.astype(BF16)

    @pl.loop(1, n_z)
    def _(s):
        gather_copy(HIDDEN, hidden, other_z(s), my_z).start()

    @pl.loop(0, n_z)
    def _(s):
        z = other_z(s)

        @pl.when(s > 0)
        def _():
            gather_copy(HIDDEN, hidden, z, z).wait_recv()

        stage[shard_rows(z), :] = contract(hidden[shard_rows(z), :], w_down[...], 1, 0).astype(BF16)
        send_blocks(OUTPUT, returned, z)

    @pl.loop(0, n_z)
    def _(z):
        wait_blocks(OUTPUT, returned, z)

    combined = gate_w[:, 0:1] * contract(gather_matrix(0).astype(BF16), returned[...], 1, 0)
    combined = combined + gate_w[:, 1:2] * contract(
        gather_matrix(1).astype(BF16), returned[...], 1, 0
    )
    mixed[...] = combined.astype(BF16)
    row_grad = level_w[...] * (combined - tgt[...].astype(F32))
    slot_grad[0] = (gate_w[:, 0:1] * row_grad).astype(BF16)
    slot_grad[1] = (gate_w[:, 1:2] * row_grad).astype(BF16)
    wait_sent(OUTPUT, returned)

    @pl.loop(0, n_z)
    def _(s):
        z = other_z(s + 1)
        value = contract(scatter_tile(z, 0).astype(BF16), slot_grad[0], 1, 0)
        value = value + contract(scatter_tile(z, 1).astype(BF16), slot_grad[1], 1, 0)
        stage[shard_rows(z), :] = value.astype(BF16)
        send_blocks(GRAD, grads, z)

    @pl.loop(1, n_z)
    def _(s):
        z = other_z(s)
        z_copy(GATE, pre_out.at[GATE, z], pre_in.at[GATE, my_z], z, my_z).wait_send()
        wait_blocks(GRAD, grads, z)
        pre_out[GATE, z] = contract(grads[shard_rows(z), :], w_down[...], 1, 1).astype(BF16)
        z_copy(HIDDEN_GRAD, pre_out.at[GATE, z], grad_in.at[my_z], z, my_z).start()

    wait_blocks(GRAD, grads, my_z)
    grad_own[...] = contract(grads[shard_rows(my_z), :], w_down[...], 1, 1)
    wait_sent(GRAD, grads)

    def tile_copy(result, c, size):
        rows = pl.ds(pl.multiple_of(c * size, size), size)
        slot = lax.rem(c, 2)
        return pltpu.make_async_copy(tiles.at[slot], result.at[rows], tile_sem.at[slot])

    def weight_grad(result, left, right):
        size = tiles.shape[1]
        count = left.shape[1] // size

        @pl.loop(0, count)
        def _(c):
            @pl.when(c >= 2)
            def _():
                tile_copy(result, c - 2, size).wait()

            columns = pl.ds(pl.multiple_of(c * size, size), size)
            tiles[lax.rem(c, 2)] = contract(left[:, columns], right[...], 0, 0)
            tile_copy(result, c, size).start()

        @pl.loop(max(count - 2, 0), count)
        def _(c):
            tile_copy(result, c, size).wait()

    weight_grad(down_grad, hidden, grads)

    @pl.loop(1, n_z)
    def _(s):
        z = other_z(s)
        z_copy(HIDDEN_GRAD, pre_out.at[GATE, z], grad_in.at[z], z, z).wait_recv()

        @pl.loop(0, shard // step)
        def _(c):
            rows = pl.ds(pl.multiple_of(c * step, step), step)
            grad_own[rows, :] = grad_own[rows, :] + grad_in[z, rows, :].astype(F32)

    @pl.loop(0, shard // step)
    def _(c):
        rows = pl.ds(pl.multiple_of(c * step, step), step)
        target = pl.ds(pl.multiple_of(my_z * shard + c * step, step), step)
        gate = gate_own[rows, :]
        grad = grad_own[rows, :]
        sigmoid = jax.nn.sigmoid(gate)
        delta = grad * up_own[rows, :] * sigmoid * (1.0 + gate * (1.0 - sigmoid))
        gate_delta[target, :] = delta.astype(BF16)
        up_delta[target, :] = (grad * gate * sigmoid).astype(BF16)

    @pl.loop(1, n_z)
    def _(s):
        gather_copy(GATE_DELTA, gate_delta, other_z(s), my_z).start()
        gather_copy(UP_DELTA, up_delta, other_z(s), my_z).start()

    @pl.loop(0, n_z)
    def _(s):
        z = other_z(s)

        @pl.when(s > 0)
        def _():
            gather_copy(GATE_DELTA, gate_delta, z, z).wait_recv()
            gather_copy(UP_DELTA, up_delta, z, z).wait_recv()

        value = contract(gate_delta[shard_rows(z), :], w_gate[...], 1, 1)
        value = value + contract(up_delta[shard_rows(z), :], w_up[...], 1, 1)
        stage[shard_rows(z), :] = value.astype(BF16)
        send_blocks(INPUT, back, z)

    weight_grad(gate_grad, arrived, gate_delta)
    weight_grad(up_grad, arrived, up_delta)

    @pl.loop(0, n_z)
    def _(z):
        wait_blocks(INPUT, back, z)

    both = (gather_matrix(0) + gather_matrix(1)).astype(BF16)
    token_grad[...] = contract(both, back[...], 1, 0).astype(BF16)
    wait_sent(INPUT, back)

    @pl.loop(1, n_z)
    def _(s):
        z = other_z(s)
        z_copy(UP, pre_out.at[UP, z], pre_in.at[UP, my_z], z, my_z).wait_send()
        z_copy(HIDDEN_GRAD, pre_out.at[GATE, z], grad_in.at[my_z], z, my_z).wait_send()
        gather_copy(HIDDEN, hidden, z, my_z).wait_send()
        gather_copy(GATE_DELTA, gate_delta, z, my_z).wait_send()
        gather_copy(UP_DELTA, up_delta, z, my_z).wait_send()


def shards(tokens, targets, expert_ids, gate_weights, level_weights, w_gate, w_up, w_down):
    n_e = lax.axis_size("expert")
    n_z = lax.axis_size("dp")
    tok_rows, quarter = tokens.shape
    ff = w_gate.shape[2]
    cap = 4 * tok_rows // n_e
    rows_all = n_e * cap
    shard = rows_all // n_z

    listed = expert_ids.reshape(-1)
    onehot = (listed[:, None] == jnp.arange(n_e, dtype=jnp.int32)[None, :]).astype(BF16)
    places = jnp.arange(2 * tok_rows, dtype=jnp.int32)
    before = (places[None, :] < places[:, None]).astype(BF16)
    earlier = contract(before, onehot, 1, 0)
    ranks = jnp.sum(earlier * onehot.astype(F32), axis=1).astype(jnp.int32)
    slots = (listed * cap + ranks).reshape(tok_rows, 2)

    vmem = pl.BlockSpec(memory_space=pltpu.VMEM)
    hbm = pl.BlockSpec(memory_space=pl.ANY)
    tile = min(256, quarter, ff)
    outs = pl.pallas_call(
        functools.partial(layer, n_z, n_e, cap),
        out_shape=(
            jax.ShapeDtypeStruct((tok_rows, quarter), BF16),
            jax.ShapeDtypeStruct((tok_rows, quarter), BF16),
            jax.ShapeDtypeStruct((quarter, ff), F32),
            jax.ShapeDtypeStruct((quarter, ff), F32),
            jax.ShapeDtypeStruct((ff, quarter), F32),
        ),
        in_specs=[vmem] * 9,
        out_specs=(vmem, vmem, hbm, hbm, hbm),
        scratch_shapes=[
            pltpu.VMEM((rows_all, quarter), BF16),
            pltpu.VMEM((rows_all, quarter), BF16),
            pltpu.VMEM((2, n_z, shard, ff), BF16),
            pltpu.VMEM((2, n_z, shard, ff), BF16),
            pltpu.VMEM((shard, ff), F32),
            pltpu.VMEM((shard, ff), F32),
            pltpu.VMEM((rows_all, ff), BF16),
            pltpu.VMEM((rows_all, quarter), BF16),
            pltpu.VMEM((2, tok_rows, quarter), BF16),
            pltpu.VMEM((rows_all, quarter), BF16),
            pltpu.VMEM((shard, ff), F32),
            pltpu.VMEM((n_z, shard, ff), BF16),
            pltpu.VMEM((rows_all, ff), BF16),
            pltpu.VMEM((rows_all, ff), BF16),
            pltpu.VMEM((rows_all, quarter), BF16),
            pltpu.VMEM((2, tile, max(ff, quarter)), F32),
            pltpu.SemaphoreType.DMA((4, n_e)),
            pltpu.SemaphoreType.DMA((4, n_e)),
            pltpu.SemaphoreType.DMA((6, n_z)),
            pltpu.SemaphoreType.DMA((6, n_z)),
            pltpu.SemaphoreType.DMA((2,)),
        ],
        compiler_params=pltpu.CompilerParams(
            collective_id=0, has_side_effects=True, vmem_limit_bytes=60 * 1024 * 1024
        ),
        cost_estimate=pl.CostEstimate(
            flops=18 * rows_all * quarter * ff, bytes_accessed=20 * quarter * ff, transcendentals=0
        ),
    )(
        tokens,
        targets,
        slots,
        slots.T,
        gate_weights,
        level_weights[:, None],
        w_gate[0],
        w_up[0],
        w_down[0],
    )
    mixed, token_grad, gate_grad, up_grad, down_grad = outs
    return (mixed, token_grad, gate_grad[None], up_grad[None], down_grad[None])


def solution(mesh):
    in_specs = (
        P("expert", "dp"),
        P("expert", "dp"),
        P("expert", None),
        P("expert", None),
        P("expert"),
        P("expert", "dp", None),
        P("expert", "dp", None),
        P("expert", None, "dp"),
    )
    out_specs = (
        P("expert", "dp"),
        P("expert", "dp"),
        P("expert", "dp", None),
        P("expert", "dp", None),
        P("expert", None, "dp"),
    )
    return jax.shard_map(shards, mesh=mesh, in_specs=in_specs, out_specs=out_specs, check_vma=False)
```

time: 672 us -> 378 us (0.56)
  the two profiles are of different devices: /device:TPU:0 before, /device:TPU:9 now
where the time goes in v1:
time: 378 us; the launch traced here: 376 us
  Pallas kernels  355 us (94%)
  local copies, waits for them, and re-layouts  19.3 us (5%)
    pallas_call x1, Pallas kernels, shards(): pl.pallas_call(functools.partial(layer, n_z, n_e, cap), out_shape=(jax.Sh...  355 us
    unnamed x13, local copies, waits for them, and re-layouts  16.7 us

profile of v1, /device:TPU:9, one launch (start us, length us, event | category | flops | bytes accessed | tf_op | source)
XLA Modules:
  0.0 376.0 jit_solution(13718121784288485417)
XLA Ops:
  0.6 1.5 copy.18.gate_w
  2.1 1.5 copy.19.level_w
  3.6 0.8 copy.15
  4.4 0.1 eq.15
  4.5 0.3 fusion
  4.8 0.1 convert_element_type.17
  5.0 0.1 copy.16
  5.0 0.7 multiply_add_fusion
  5.7 0.0 copy-start.2
  5.7 0.8 copy.17.slot_cols
  6.5 0.0 copy-done.2
  6.6 355.0 %shard_map.119 = (bf16[256,1024]{1,0:T(8,128)(2,1)}, bf16[256,1024]{1,0:T(8,128)(2,1)}, f32[1024,1024]{1,0:T(8,128)}, f32[1024,1024]{1,0:T(8,128)}, f32[1024,1024]{1,0:T(8,128)}) custom-call(bf16[256,1024]{1,0:T(8,128)(2,1)} %tok.1, bf16[256,1024]{1,0:T(8,128)(2,1)} %tgt.1, s32[256,2]{1,0:T(8,128)} %copy.17.slot_cols, s32[2,256]{1,0:T(2,128)} %bitcast.11, ...), custom_call_target="tpu_custom_call" | custom-call | flops 19327352832 | bytes 20971520 | tf_op jit(solution)/shard_map/pallas_call | solution.py:349
  361.6 1.9 copy.25
  363.5 1.9 copy.26
  365.3 0.0 copy-start.1
  365.3 4.9 %copy.27 = f32[1,1024,1024]{2,1,0:T(8,128)} copy(f32[1,1024,1024]{2,1,0:T(8,128)} %bitcast.10) | data formatting | bytes 8388608
  370.3 0.0 copy-done.1
  370.3 0.0 copy-start
  370.3 2.1 copy.28
  372.4 1.6 copy-done
  374.0 2.0 copy.29
  (1 shorter events, 0.0 us)
Async XLA Ops:
  5.7 0.8 copy-start.2
  365.3 4.9 %copy-start.1 = (f32[1024,1024]{1,0:T(8,128)S(1)}, f32[1024,1024]{1,0:T(8,128)}, u32[]{:S(2)}) copy-start(f32[1024,1024]{1,0:T(8,128)} %get-tuple-element.13) | copy-start | bytes 12582916
  370.3 3.7 copy-start

commit v2 on v1

v2 whole, which is shorter than its diff:
```python
import functools

import jax
import jax.numpy as jnp
from jax import lax
from jax.experimental import pallas as pl
from jax.experimental.pallas import tpu as pltpu
from jax.sharding import PartitionSpec as P

BF16 = jnp.bfloat16
F32 = jnp.float32
MESH = pl.DeviceIdType.MESH

HALVES = 2

DISPATCH, OUTPUT, GRAD, INPUT = range(4)
GATE, UP, HIDDEN, HIDDEN_GRAD, GATE_DELTA, UP_DELTA = range(6)


def contract(left, right, left_dim, right_dim):
    return lax.dot_general(
        left, right, (((left_dim,), (right_dim,)), ((), ())), preferred_element_type=F32
    )


def layer(
    n_z,
    n_e,
    cap,
    tok,
    tgt,
    slot_cols,
    slot_lanes,
    gate_w,
    level_w,
    w_gate,
    w_up,
    w_down,
    mixed,
    token_grad,
    gate_grad,
    up_grad,
    down_grad,
    stage,
    arrived,
    pre_out,
    pre_in,
    gate_own,
    up_own,
    hidden,
    returned,
    slot_grad,
    grads,
    grad_own,
    grad_in,
    gate_delta,
    up_delta,
    back,
    tiles,
    e_send,
    e_recv,
    z_send,
    z_recv,
    tile_sem,
):
    my_z = lax.axis_index("dp")
    my_e = lax.axis_index("expert")
    rows_all = n_e * cap
    part = cap // HALVES
    half_rows = n_e * part
    shard = half_rows // n_z
    per_shard = n_e // n_z
    tok_rows = tok.shape[0]
    step = min(64, shard)

    def shard_rows(h, z):
        return pl.ds(pl.multiple_of(h * half_rows + z * shard, shard), shard)

    def block_rows(h, e):
        return pl.ds(pl.multiple_of(h * half_rows + e * part, part), part)

    def e_copy(phase, h, landing, other, source):
        return pltpu.make_async_remote_copy(
            src_ref=stage.at[block_rows(h, other)],
            dst_ref=landing.at[block_rows(h, source)],
            send_sem=e_send.at[phase, h, other],
            recv_sem=e_recv.at[phase, h, source],
            device_id={"expert": other},
            device_id_type=MESH,
        )

    def send_blocks(phase, h, landing, z):
        for i in range(per_shard):
            other = z * per_shard + i

            @pl.when(other != my_e)
            def _():
                e_copy(phase, h, landing, other, my_e).start()

            @pl.when(other == my_e)
            def _():
                landing[block_rows(h, my_e), :] = stage[block_rows(h, my_e), :]

    def wait_blocks(phase, h, landing, z):
        for i in range(per_shard):
            other = z * per_shard + i

            @pl.when(other != my_e)
            def _():
                e_copy(phase, h, landing, other, other).wait_recv()

    def wait_sent(phase, h, landing):
        @pl.loop(0, n_e)
        def _(other):
            @pl.when(other != my_e)
            def _():
                e_copy(phase, h, landing, other, my_e).wait_send()

    def z_copy(phase, h, src, dst, z, source):
        return pltpu.make_async_remote_copy(
            src_ref=src,
            dst_ref=dst,
            send_sem=z_send.at[phase, h, z],
            recv_sem=z_recv.at[phase, h, source],
            device_id={"dp": z},
            device_id_type=MESH,
        )

    def gather_copy(phase, h, array, z, source):
        rows = array.at[shard_rows(h, source)]
        return z_copy(phase, h, rows, rows, z, source)

    def sum_copy(phase, h, z, source):
        if phase == HIDDEN_GRAD:
            return z_copy(phase, h, pre_out.at[GATE, h, z], grad_in.at[h, source], z, source)
        return z_copy(phase, h, pre_out.at[phase, h, z], pre_in.at[phase, h, source], z, source)

    def other_z(s):
        return lax.rem(my_z + s, n_z)

    barrier = pltpu.get_barrier_semaphore()

    @pl.loop(1, n_z)
    def _(s):
        pl.semaphore_signal(barrier, inc=1, device_id={"dp": other_z(s)}, device_id_type=MESH)

    @pl.loop(1, n_e)
    def _(s):
        pl.semaphore_signal(
            barrier, inc=1, device_id={"expert": lax.rem(my_e + s, n_e)}, device_id_type=MESH
        )

    pl.semaphore_wait(barrier, n_z + n_e - 2)

    def scatter_tile(h, z, k):
        first = h * half_rows + z * shard
        slots = lax.broadcasted_iota(jnp.int32, (shard, tok_rows), 0) + first
        return (slots == slot_lanes[k : k + 1, :]).astype(F32)

    def gather_matrix(k):
        slots = lax.broadcasted_iota(jnp.int32, (tok_rows, rows_all), 1)
        return (slots == slot_cols[:, k : k + 1]).astype(F32)

    for h in range(HALVES):

        @pl.loop(0, n_z)
        def _(s):
            z = other_z(s + 1)
            chosen = (scatter_tile(h, z, 0) + scatter_tile(h, z, 1)).astype(BF16)
            stage[shard_rows(h, z), :] = contract(chosen, tok[...], 1, 0).astype(BF16)
            send_blocks(DISPATCH, h, arrived, z)

    for h in range(HALVES):

        @pl.loop(1, n_z)
        def _(s):
            z = other_z(s)
            wait_blocks(DISPATCH, h, arrived, z)
            rows = arrived[shard_rows(h, z), :]
            pre_out[GATE, h, z] = contract(rows, w_gate[...], 1, 0).astype(BF16)
            sum_copy(GATE, h, z, my_z).start()
            pre_out[UP, h, z] = contract(rows, w_up[...], 1, 0).astype(BF16)
            sum_copy(UP, h, z, my_z).start()

        wait_blocks(DISPATCH, h, arrived, my_z)
        gate_own[h] = contract(arrived[shard_rows(h, my_z), :], w_gate[...], 1, 0)
        up_own[h] = contract(arrived[shard_rows(h, my_z), :], w_up[...], 1, 0)

    def add_arrived(phase, h, own, landing):
        @pl.loop(1, n_z)
        def _(s):
            z = other_z(s)
            sum_copy(phase, h, z, z).wait_recv()

            @pl.loop(0, shard // step)
            def _(c):
                rows = pl.ds(pl.multiple_of(c * step, step), step)
                own[h, rows, :] = own[h, rows, :] + landing[h, z, rows, :].astype(F32)

    for h in range(HALVES):
        add_arrived(GATE, h, gate_own, pre_in.at[GATE])
        add_arrived(UP, h, up_own, pre_in.at[UP])

        @pl.loop(0, shard // step)
        def _(c):
            rows = pl.ds(pl.multiple_of(c * step, step), step)
            gate = gate_own[h, rows, :]
            value = gate * jax.nn.sigmoid(gate) * up_own[h, rows, :]
            first = h * half_rows + my_z * shard + c * step
            hidden[pl.ds(pl.multiple_of(first, step), step), :] = value.astype(BF16)

        @pl.loop(1, n_z)
        def _(s):
            gather_copy(HIDDEN, h, hidden, other_z(s), my_z).start()

    for h in range(HALVES):
        wait_sent(DISPATCH, h, arrived)

        @pl.loop(0, n_z)
        def _(s):
            z = other_z(s)

            @pl.when(s > 0)
            def _():
                gather_copy(HIDDEN, h, hidden, z, z).wait_recv()

            rows = hidden[shard_rows(h, z), :]
            stage[shard_rows(h, z), :] = contract(rows, w_down[...], 1, 0).astype(BF16)
            send_blocks(OUTPUT, h, returned, z)

    for h in range(HALVES):

        @pl.loop(0, n_z)
        def _(z):
            wait_blocks(OUTPUT, h, returned, z)

    combined = gate_w[:, 0:1] * contract(gather_matrix(0).astype(BF16), returned[...], 1, 0)
    combined = combined + gate_w[:, 1:2] * contract(
        gather_matrix(1).astype(BF16), returned[...], 1, 0
    )
    mixed[...] = combined.astype(BF16)
    row_grad = level_w[...] * (combined - tgt[...].astype(F32))
    slot_grad[0] = (gate_w[:, 0:1] * row_grad).astype(BF16)
    slot_grad[1] = (gate_w[:, 1:2] * row_grad).astype(BF16)

    for h in range(HALVES):
        wait_sent(OUTPUT, h, returned)

        @pl.loop(0, n_z)
        def _(s):
            z = other_z(s + 1)
            value = contract(scatter_tile(h, z, 0).astype(BF16), slot_grad[0], 1, 0)
            value = value + contract(scatter_tile(h, z, 1).astype(BF16), slot_grad[1], 1, 0)
            stage[shard_rows(h, z), :] = value.astype(BF16)
            send_blocks(GRAD, h, grads, z)

    for h in range(HALVES):

        @pl.loop(1, n_z)
        def _(s):
            z = other_z(s)
            sum_copy(GATE, h, z, my_z).wait_send()
            wait_blocks(GRAD, h, grads, z)
            rows = grads[shard_rows(h, z), :]
            pre_out[GATE, h, z] = contract(rows, w_down[...], 1, 1).astype(BF16)
            sum_copy(HIDDEN_GRAD, h, z, my_z).start()

        wait_blocks(GRAD, h, grads, my_z)
        grad_own[h] = contract(grads[shard_rows(h, my_z), :], w_down[...], 1, 1)

    def tile_copy(result, c, size):
        rows = pl.ds(pl.multiple_of(c * size, size), size)
        slot = lax.rem(c, 2)
        return pltpu.make_async_copy(tiles.at[slot], result.at[rows], tile_sem.at[slot])

    def weight_grad(result, left, right):
        size = tiles.shape[1]
        count = left.shape[1] // size

        @pl.loop(0, count)
        def _(c):
            @pl.when(c >= 2)
            def _():
                tile_copy(result, c - 2, size).wait()

            columns = pl.ds(pl.multiple_of(c * size, size), size)
            tiles[lax.rem(c, 2)] = contract(left[:, columns], right[...], 0, 0)
            tile_copy(result, c, size).start()

        @pl.loop(max(count - 2, 0), count)
        def _(c):
            tile_copy(result, c, size).wait()

    weight_grad(down_grad, hidden, grads)

    for h in range(HALVES):
        add_arrived(HIDDEN_GRAD, h, grad_own, grad_in)

        @pl.loop(0, shard // step)
        def _(c):
            rows = pl.ds(pl.multiple_of(c * step, step), step)
            first = h * half_rows + my_z * shard + c * step
            target = pl.ds(pl.multiple_of(first, step), step)
            gate = gate_own[h, rows, :]
            grad = grad_own[h, rows, :]
            sigmoid = jax.nn.sigmoid(gate)
            delta = grad * up_own[h, rows, :] * sigmoid * (1.0 + gate * (1.0 - sigmoid))
            gate_delta[target, :] = delta.astype(BF16)
            up_delta[target, :] = (grad * gate * sigmoid).astype(BF16)

        @pl.loop(1, n_z)
        def _(s):
            gather_copy(GATE_DELTA, h, gate_delta, other_z(s), my_z).start()
            gather_copy(UP_DELTA, h, up_delta, other_z(s), my_z).start()

    for h in range(HALVES):
        wait_sent(GRAD, h, grads)

        @pl.loop(0, n_z)
        def _(s):
            z = other_z(s)

            @pl.when(s > 0)
            def _():
                gather_copy(GATE_DELTA, h, gate_delta, z, z).wait_recv()
                gather_copy(UP_DELTA, h, up_delta, z, z).wait_recv()

            value = contract(gate_delta[shard_rows(h, z), :], w_gate[...], 1, 1)
            value = value + contract(up_delta[shard_rows(h, z), :], w_up[...], 1, 1)
            stage[shard_rows(h, z), :] = value.astype(BF16)
            send_blocks(INPUT, h, back, z)

    weight_grad(gate_grad, arrived, gate_delta)
    weight_grad(up_grad, arrived, up_delta)

    for h in range(HALVES):

        @pl.loop(0, n_z)
        def _(z):
            wait_blocks(INPUT, h, back, z)

    both = (gather_matrix(0) + gather_matrix(1)).astype(BF16)
    token_grad[...] = contract(both, back[...], 1, 0).astype(BF16)

    for h in range(HALVES):
        wait_sent(INPUT, h, back)

        @pl.loop(1, n_z)
        def _(s):
            z = other_z(s)
            sum_copy(UP, h, z, my_z).wait_send()
            sum_copy(HIDDEN_GRAD, h, z, my_z).wait_send()
            gather_copy(HIDDEN, h, hidden, z, my_z).wait_send()
            gather_copy(GATE_DELTA, h, gate_delta, z, my_z).wait_send()
            gather_copy(UP_DELTA, h, up_delta, z, my_z).wait_send()


def shards(tokens, targets, expert_ids, gate_weights, level_weights, w_gate, w_up, w_down):
    n_e = lax.axis_size("expert")
    n_z = lax.axis_size("dp")
    tok_rows, quarter = tokens.shape
    ff = w_gate.shape[2]
    cap = 4 * tok_rows // n_e
    rows_all = n_e * cap
    part = cap // HALVES
    shard = n_e * part // n_z

    listed = expert_ids.reshape(-1)
    onehot = (listed[:, None] == jnp.arange(n_e, dtype=jnp.int32)[None, :]).astype(BF16)
    places = jnp.arange(2 * tok_rows, dtype=jnp.int32)
    before = (places[None, :] < places[:, None]).astype(BF16)
    earlier = contract(before, onehot, 1, 0)
    ranks = jnp.sum(earlier * onehot.astype(F32), axis=1).astype(jnp.int32)
    slots = ranks // part * (n_e * part) + listed * part + ranks % part
    slots = slots.reshape(tok_rows, 2)

    vmem = pl.BlockSpec(memory_space=pltpu.VMEM)
    hbm = pl.BlockSpec(memory_space=pl.ANY)
    tile = min(256, quarter, ff)
    outs = pl.pallas_call(
        functools.partial(layer, n_z, n_e, cap),
        out_shape=(
            jax.ShapeDtypeStruct((tok_rows, quarter), BF16),
            jax.ShapeDtypeStruct((tok_rows, quarter), BF16),
            jax.ShapeDtypeStruct((quarter, ff), F32),
            jax.ShapeDtypeStruct((quarter, ff), F32),
            jax.ShapeDtypeStruct((ff, quarter), F32),
        ),
        in_specs=[vmem] * 9,
        out_specs=(vmem, vmem, hbm, hbm, hbm),
        scratch_shapes=[
            pltpu.VMEM((rows_all, quarter), BF16),
            pltpu.VMEM((rows_all, quarter), BF16),
            pltpu.VMEM((2, HALVES, n_z, shard, ff), BF16),
            pltpu.VMEM((2, HALVES, n_z, shard, ff), BF16),
            pltpu.VMEM((HALVES, shard, ff), F32),
            pltpu.VMEM((HALVES, shard, ff), F32),
            pltpu.VMEM((rows_all, ff), BF16),
            pltpu.VMEM((rows_all, quarter), BF16),
            pltpu.VMEM((2, tok_rows, quarter), BF16),
            pltpu.VMEM((rows_all, quarter), BF16),
            pltpu.VMEM((HALVES, shard, ff), F32),
            pltpu.VMEM((HALVES, n_z, shard, ff), BF16),
            pltpu.VMEM((rows_all, ff), BF16),
            pltpu.VMEM((rows_all, ff), BF16),
            pltpu.VMEM((rows_all, quarter), BF16),
            pltpu.VMEM((2, tile, max(ff, quarter)), F32),
            pltpu.SemaphoreType.DMA((4, HALVES, n_e)),
            pltpu.SemaphoreType.DMA((4, HALVES, n_e)),
            pltpu.SemaphoreType.DMA((6, HALVES, n_z)),
            pltpu.SemaphoreType.DMA((6, HALVES, n_z)),
            pltpu.SemaphoreType.DMA((2,)),
        ],
        compiler_params=pltpu.CompilerParams(
            collective_id=0, has_side_effects=True, vmem_limit_bytes=60 * 1024 * 1024
        ),
        cost_estimate=pl.CostEstimate(
            flops=18 * rows_all * quarter * ff, bytes_accessed=20 * quarter * ff, transcendentals=0
        ),
    )(
        tokens,
        targets,
        slots,
        slots.T,
        gate_weights,
        level_weights[:, None],
        w_gate[0],
        w_up[0],
        w_down[0],
    )
    mixed, token_grad, gate_grad, up_grad, down_grad = outs
    return (mixed, token_grad, gate_grad[None], up_grad[None], down_grad[None])


def solution(mesh):
    in_specs = (
        P("expert", "dp"),
        P("expert", "dp"),
        P("expert", None),
        P("expert", None),
        P("expert"),
        P("expert", "dp", None),
        P("expert", "dp", None),
        P("expert", None, "dp"),
    )
    out_specs = (
        P("expert", "dp"),
        P("expert", "dp"),
        P("expert", "dp", None),
        P("expert", "dp", None),
        P("expert", None, "dp"),
    )
    return jax.shard_map(shards, mesh=mesh, in_specs=in_specs, out_specs=out_specs, check_vma=False)
```

time: 378 us -> 351 us (0.929)
  Pallas kernels: 355 us -> 330 us
    pallas_call x1, Pallas kernels: 355 us -> 330 us  [shards(): pl.pallas_call(functools.partial(layer, n_z, n_e, cap), out_shape=(jax.Sh...]
where the time goes in v2:
time: 351 us
  Pallas kernels  330 us (94%)
  local copies, waits for them, and re-layouts  19.3 us (5%)
    pallas_call x1, Pallas kernels, shards(): pl.pallas_call(functools.partial(layer, n_z, n_e, cap), out_shape=(jax.Sh...  330 us
    unnamed x13, local copies, waits for them, and re-layouts  16.7 us

profile of v2, /device:TPU:9, one launch (start us, length us, event | category | flops | bytes accessed | tf_op | source)
XLA Modules:
  0.0 350.8 jit_solution(11444163664937792406)
XLA Ops:
  0.6 1.5 copy.21.gate_w
  2.1 1.5 copy.22.level_w
  3.6 0.8 copy.15
  4.4 0.1 eq.17
  4.5 0.3 fusion
  4.8 0.1 convert_element_type.17
  5.0 0.1 copy.16
  5.0 0.7 fusion.3
  5.8 0.0 copy-start.2
  5.8 0.8 copy.20.slot_cols
  6.6 0.0 copy-done.2
  6.6 329.8 %shard_map.119 = (bf16[256,1024]{1,0:T(8,128)(2,1)}, bf16[256,1024]{1,0:T(8,128)(2,1)}, f32[1024,1024]{1,0:T(8,128)}, f32[1024,1024]{1,0:T(8,128)}, f32[1024,1024]{1,0:T(8,128)}) custom-call(bf16[256,1024]{1,0:T(8,128)(2,1)} %tok.1, bf16[256,1024]{1,0:T(8,128)(2,1)} %tgt.1, s32[256,2]{1,0:T(8,128)} %copy.20.slot_cols, s32[2,256]{1,0:T(2,128)} %bitcast.11, ...), custom_call_target="tpu_custom_call" | custom-call | flops 19327352832 | bytes 20971520 | tf_op jit(solution)/shard_map/pallas_call | solution.py:380
  336.4 1.9 copy.28
  338.3 1.9 copy.29
  340.1 0.0 copy-start.1
  340.2 4.9 %copy.30 = f32[1,1024,1024]{2,1,0:T(8,128)} copy(f32[1,1024,1024]{2,1,0:T(8,128)} %bitcast.10) | data formatting | bytes 8388608
  345.1 0.0 copy-done.1
  345.1 0.0 copy-start
  345.1 2.1 copy.31
  347.2 1.6 copy-done
  348.8 2.0 copy.32
  (1 shorter events, 0.0 us)
Async XLA Ops:
  5.8 0.8 copy-start.2
  340.1 4.9 %copy-start.1 = (f32[1024,1024]{1,0:T(8,128)S(1)}, f32[1024,1024]{1,0:T(8,128)}, u32[]{:S(2)}) copy-start(f32[1024,1024]{1,0:T(8,128)} %get-tuple-element.13) | copy-start | bytes 12582916
  345.1 3.7 %copy-start = (f32[1024,1024]{1,0:T(8,128)S(1)}, f32[1024,1024]{1,0:T(8,128)}, u32[]{:S(2)}) copy-start(f32[1024,1024]{1,0:T(8,128)} %get-tuple-element.14) | copy-start | bytes 12582916

commit v3 on v2

--- a/solution.py
+++ b/solution.py
@@ -56,11 +56,13 @@
     gate_delta,
     up_delta,
     back,
+    relay_in,
     tiles,
     e_send,
     e_recv,
     z_send,
     z_recv,
+    relay_recv,
     tile_sem,
 ):
     my_z = lax.axis_index("dp")
@@ -138,6 +140,54 @@
     def other_z(s):
         return lax.rem(my_z + s, n_z)
 
+    relay = n_z == 4
+
+    def send_place(i):
+        if not relay:
+            return other_z(i + 1)
+        upper, last = my_z // 2, i // 2
+        return other_z((1 - last) * (3 - 2 * upper + lax.rem(i, 2) * (4 * upper - 2)) + 2 * last)
+
+    def far(z):
+        return (my_z - z) * (my_z - z) == 9
+
+    def relay_copy(phase, h, z):
+        slot = 2 if phase == HIDDEN_GRAD else phase
+        return pltpu.make_async_remote_copy(
+            src_ref=pre_out.at[phase % HIDDEN_GRAD, h, z],
+            dst_ref=relay_in.at[slot, h],
+            send_sem=z_send.at[phase, h, z],
+            recv_sem=relay_recv.at[slot, h],
+            device_id={"dp": 1 + my_z // 3},
+            device_id_type=MESH,
+        )
+
+    def send_sum(phase, h, i, z, value):
+        out = pre_out.at[phase % HIDDEN_GRAD, h, z]
+        if not relay:
+            out[...] = value.astype(BF16)
+            sum_copy(phase, h, z, my_z).start()
+            return
+        adds = (i // 2) * lax.rem(my_z, 3)
+
+        @pl.when(adds == 0)
+        def _():
+            out[...] = value.astype(BF16)
+
+        @pl.when(adds != 0)
+        def _():
+            relay_copy(phase, h, z).wait_recv()
+            slot = 2 if phase == HIDDEN_GRAD else phase
+            out[...] = (value + relay_in[slot, h].astype(F32)).astype(BF16)
+
+        @pl.when(far(z))
+        def _():
+            relay_copy(phase, h, z).start()
+
+        @pl.when(jnp.logical_not(far(z)))
+        def _():
+            sum_copy(phase, h, z, my_z).start()
+
     barrier = pltpu.get_barrier_semaphore()
 
     @pl.loop(1, n_z)
@@ -172,15 +222,13 @@
 
     for h in range(HALVES):
 
-        @pl.loop(1, n_z)
-        def _(s):
-            z = other_z(s)
+        @pl.loop(0, n_z - 1)
+        def _(i):
+            z = send_place(i)
             wait_blocks(DISPATCH, h, arrived, z)
             rows = arrived[shard_rows(h, z), :]
-            pre_out[GATE, h, z] = contract(rows, w_gate[...], 1, 0).astype(BF16)
-            sum_copy(GATE, h, z, my_z).start()
-            pre_out[UP, h, z] = contract(rows, w_up[...], 1, 0).astype(BF16)
-            sum_copy(UP, h, z, my_z).start()
+            send_sum(GATE, h, i, z, contract(rows, w_gate[...], 1, 0))
+            send_sum(UP, h, i, z, contract(rows, w_up[...], 1, 0))
 
         wait_blocks(DISPATCH, h, arrived, my_z)
         gate_own[h] = contract(arrived[shard_rows(h, my_z), :], w_gate[...], 1, 0)
@@ -190,12 +238,15 @@
         @pl.loop(1, n_z)
         def _(s):
             z = other_z(s)
-            sum_copy(phase, h, z, z).wait_recv()
-
-            @pl.loop(0, shard // step)
-            def _(c):
-                rows = pl.ds(pl.multiple_of(c * step, step), step)
-                own[h, rows, :] = own[h, rows, :] + landing[h, z, rows, :].astype(F32)
+
+            @pl.when(jnp.logical_not(far(z)) if relay else s > 0)
+            def _():
+                sum_copy(phase, h, z, z).wait_recv()
+
+                @pl.loop(0, shard // step)
+                def _(c):
+                    rows = pl.ds(pl.multiple_of(c * step, step), step)
+                    own[h, rows, :] = own[h, rows, :] + landing[h, z, rows, :].astype(F32)
 
     for h in range(HALVES):
         add_arrived(GATE, h, gate_own, pre_in.at[GATE])
@@ -256,14 +307,13 @@
 
     for h in range(HALVES):
 
-        @pl.loop(1, n_z)
-        def _(s):
-            z = other_z(s)
+        @pl.loop(0, n_z - 1)
+        def _(i):
+            z = send_place(i)
             sum_copy(GATE, h, z, my_z).wait_send()
             wait_blocks(GRAD, h, grads, z)
             rows = grads[shard_rows(h, z), :]
-            pre_out[GATE, h, z] = contract(rows, w_down[...], 1, 1).astype(BF16)
-            sum_copy(HIDDEN_GRAD, h, z, my_z).start()
+            send_sum(HIDDEN_GRAD, h, i, z, contract(rows, w_down[...], 1, 1))
 
         wait_blocks(GRAD, h, grads, my_z)
         grad_own[h] = contract(grads[shard_rows(h, my_z), :], w_down[...], 1, 1)
@@ -404,11 +454,13 @@
             pltpu.VMEM((rows_all, ff), BF16),
             pltpu.VMEM((rows_all, ff), BF16),
             pltpu.VMEM((rows_all, quarter), BF16),
+            pltpu.VMEM((3, HALVES, shard, ff), BF16),
             pltpu.VMEM((2, tile, max(ff, quarter)), F32),
             pltpu.SemaphoreType.DMA((4, HALVES, n_e)),
             pltpu.SemaphoreType.DMA((4, HALVES, n_e)),
             pltpu.SemaphoreType.DMA((6, HALVES, n_z)),
             pltpu.SemaphoreType.DMA((6, HALVES, n_z)),
+            pltpu.SemaphoreType.DMA((3, HALVES)),
             pltpu.SemaphoreType.DMA((2,)),
         ],
         compiler_params=pltpu.CompilerParams(

time: 351 us -> 323 us (0.920)
  Pallas kernels: 330 us -> 301 us
    pallas_call x1, Pallas kernels: 330 us -> 301 us  [shards(): pl.pallas_call(functools.partial(layer, n_z, n_e, cap), out_shape=(jax.Sh...]
where the time goes in v3:
time: 323 us; the launch traced here: 322 us
  Pallas kernels  301 us (93%)
  local copies, waits for them, and re-layouts  19.3 us (6%)
    pallas_call x1, Pallas kernels, shards(): pl.pallas_call(functools.partial(layer, n_z, n_e, cap), out_shape=(jax.Sh...  301 us
    unnamed x13, local copies, waits for them, and re-layouts  16.7 us

profile of v3, /device:TPU:9, one launch (start us, length us, event | category | flops | bytes accessed | tf_op | source)
XLA Modules:
  0.0 322.2 jit_solution(2924052682805234308)
XLA Ops:
  0.6 1.5 copy.21.gate_w
  2.1 1.5 copy.22.level_w
  3.6 0.8 copy.15
  4.4 0.1 eq.17
  4.5 0.3 fusion
  4.8 0.1 convert_element_type.17
  5.0 0.1 copy.16
  5.0 0.7 fusion.3
  5.8 0.0 copy-start.2
  5.8 0.8 copy.20.slot_cols
  6.6 0.0 copy-done.2
  6.6 301.3 %shard_map.119 = (bf16[256,1024]{1,0:T(8,128)(2,1)}, bf16[256,1024]{1,0:T(8,128)(2,1)}, f32[1024,1024]{1,0:T(8,128)}, f32[1024,1024]{1,0:T(8,128)}, f32[1024,1024]{1,0:T(8,128)}) custom-call(bf16[256,1024]{1,0:T(8,128)(2,1)} %tok.1, bf16[256,1024]{1,0:T(8,128)(2,1)} %tgt.1, s32[256,2]{1,0:T(8,128)} %copy.20.slot_cols, s32[2,256]{1,0:T(2,128)} %bitcast.11, ...), custom_call_target="tpu_custom_call" | custom-call | flops 19327352832 | bytes 20971520 | tf_op jit(solution)/shard_map/pallas_call | solution.py:430
  307.9 1.9 copy.28
  309.7 1.9 copy.29
  311.6 0.0 copy-start.1
  311.6 4.9 %copy.30 = f32[1,1024,1024]{2,1,0:T(8,128)} copy(f32[1,1024,1024]{2,1,0:T(8,128)} %bitcast.10) | data formatting | bytes 8388608
  316.5 0.0 copy-done.1
  316.5 0.0 copy-start
  316.5 2.1 copy.31
  318.7 1.6 copy-done
  320.2 2.0 copy.32
  (1 shorter events, 0.0 us)
Async XLA Ops:
  5.8 0.8 copy-start.2
  311.6 4.9 %copy-start.1 = (f32[1024,1024]{1,0:T(8,128)S(1)}, f32[1024,1024]{1,0:T(8,128)}, u32[]{:S(2)}) copy-start(f32[1024,1024]{1,0:T(8,128)} %get-tuple-element.13) | copy-start | bytes 12582916
  316.5 3.7 %copy-start = (f32[1024,1024]{1,0:T(8,128)S(1)}, f32[1024,1024]{1,0:T(8,128)}, u32[]{:S(2)}) copy-start(f32[1024,1024]{1,0:T(8,128)} %get-tuple-element.14) | copy-start | bytes 12582916
